TPU v7x, 32 devices: a whole 2x2x4 slice. The times are simulated.
32 devices in a mesh: section: 4 (over z), dp: 4 (over y, x), tensor: 2 (over core).
Axes of the slice: x: 2, y: 2, z: 4, core: 2. Of those that a mesh axis runs over, the one named last changes fastest.
Arguments:
- grad_hidden: bfloat16 [4, 512, 16384], P('section', None, ('dp', 'tensor')), may hold values from -6 to 6
- gate_pre: bfloat16 [4, 512, 16384], P('section', None, ('dp', 'tensor')), may hold values from -6 to 6
- up_pre: bfloat16 [4, 512, 16384], P('section', None, ('dp', 'tensor')), may hold values from -6 to 6
- w_gate: bfloat16 [4, 16384, 6144], P('section', ('dp', 'tensor')), may hold values from -0.078125 to 0.078125
- w_up: bfloat16 [4, 16384, 6144], P('section', ('dp', 'tensor')), may hold values from -0.078125 to 0.078125
- block_expert: int32 [4, 4], P('section'), may hold values from 0 to 1
Outputs:
- prev_grad: bfloat16 [4, 512, 6144], P('section', ('dp', 'tensor'))
Inputs may be any that keep to these rules, and one draw needn't show every extreme that they name: block_expert[s, b] is the expert of rows b * 128 to (b + 1) * 128 - 1 of layer s.
All inputs are finite; a program needn't handle non-finite values.
Results may differ from a plain program's by a relative error of at most 0.019.
Values may be sent and summed in bfloat16 or wider, within the bound.
No kernel may reach another device: no remote copies, remote signals or barrier semaphores. Data moves between devices by JAX's collectives and lax.ppermute only.
A program may use at most 192 MiB of HBM per device.

v0:
```python
import functools

import jax
import jax.numpy as jnp
from jax import lax
from jax.experimental import pallas as pl
from jax.experimental.pallas import tpu as pltpu
from jax.sharding import PartitionSpec as P

F = 8192
BLOCK = 128
HALF = BLOCK // 2
DEPTH = 3
PLAN = (3, 4, 3, 2)
HBM = pltpu.MemorySpace.HBM
VMEM = pltpu.MemorySpace.VMEM


def swiglu_grads(grad, gate, up):
    grad = grad.astype(jnp.float32)
    gate = gate.astype(jnp.float32)
    up = up.astype(jnp.float32)
    sig = 0.5 * jnp.tanh(0.5 * gate) + 0.5
    gated = gate * sig
    grad_gate = (grad * sig) * up * (1.0 + gate - gated)
    return grad_gate.astype(jnp.bfloat16), (grad * gated).astype(jnp.bfloat16)


def parts_of(blocks, xor):
    return [(0, 2), (2, 3), (3, 4)] if xor else [(0, blocks)]


def terms_kernel(*refs, first, after_width, prepare, waits, xor):
    refs = list(refs)
    layout = refs.pop(0)
    rows = [refs.pop(0) for _ in range(3 if prepare else 1)]
    if not prepare:
        refs.pop(0)
    w_gate, w_up = refs.pop(0), refs.pop(0)
    del refs[:waits]
    ring = refs.pop(0)
    keep = refs.pop(0)
    blocks, _, width = keep.shape
    sends = [(low, high, refs.pop(0)) for low, high in parts_of(blocks, xor)]
    lhs = refs.pop(0) if prepare else rows[0]
    order, wsem = refs.pop(0), refs.pop(0)
    if prepare:
        abuf, asem = refs
    hid, columns = w_gate.shape
    depth, _, tile = ring.shape
    steps = width // tile
    ahead = 0 if prepare else 1
    wanted = steps + (1 if after_width else 0)
    part = tile // 2
    rank = lax.axis_index("dp")
    pair = lax.axis_index("tensor")
    mine = lax.div((rank * lax.axis_size("tensor") + pair) * hid, F)

    def block_of(mask):
        return lax.bitwise_xor(rank, mask) if xor else mask

    def slot_of(mask, side):
        return mask % 2 * 2 + mask // 2 if xor and side else mask

    count = jnp.int32(0)
    for mask in range(blocks):
        owned = layout[0, block_of(mask)] == mine

        @pl.when(owned)
        def _(count=count, mask=mask):
            order[count] = mask

        count = count + owned.astype(jnp.int32)

    def place_of(step):
        return lax.rem(first // tile + step, depth)

    def weight_copies(step):
        at = place_of(step)
        if isinstance(step, int) and step == steps:
            start, across = first + width, after_width // 2
        else:
            start, across = first + step * part, width // 2
        return [
            pltpu.make_async_copy(
                w.at[:, pl.ds(pl.multiple_of(start + side * across, 128), part)],
                ring.at[at, pl.ds(i * hid, hid), pl.ds(side * part, part)],
                wsem.at[at, 2 * i + side],
            )
            for i, w in enumerate((w_gate, w_up))
            for side in range(2)
        ]

    def row_copies(place):
        at = pl.ds(pl.multiple_of(block_of(order[place]) * BLOCK, BLOCK), BLOCK)
        return [
            pltpu.make_async_copy(a.at[at], abuf.at[place, i], asem.at[place, i])
            for i, a in enumerate(rows)
        ]

    def prepare_block(place, carry):
        for copy in row_copies(place):
            copy.wait()

        def rows_at(i, carry):
            at = pl.ds(pl.multiple_of(i * 16, 16), 16)
            grad_gate, grad_up = swiglu_grads(*(abuf[place, k, at] for k in range(3)))
            to = place * BLOCK + lax.rem(i * 16 + pair * HALF, BLOCK)
            to = pl.ds(pl.multiple_of(to, 16), 16)
            lhs[to, :hid] = grad_gate
            lhs[to, hid:] = grad_up
            return carry

        return lax.fori_loop(0, BLOCK // 16, rows_at, carry, unroll=2)

    def multiply(step, base, size):
        out = jnp.dot(
            lhs[pl.ds(pl.multiple_of(base * BLOCK, BLOCK), size * BLOCK)],
            ring[place_of(step)],
            preferred_element_type=jnp.float32,
        ).astype(jnp.bfloat16)
        for i in range(size):
            for side in range(2):
                slot = slot_of(order[base + i], side)
                cols = pl.ds(pl.multiple_of(side * (width // 2) + step * part, 128), part)
                mine_out, other_out = (
                    out[i * BLOCK + k * HALF : i * BLOCK + (k + 1) * HALF, side * part : side * part + part]
                    for k in range(2)
                )
                keep[slot, :, cols] = mine_out
                for low, high, send in sends:

                    @pl.when((slot >= low) & (slot < high))
                    def _(low=low, send=send, slot=slot, cols=cols, other_out=other_out):
                        send[slot - low, :, cols] = other_out

    def one_tile(step, carry):
        @pl.when(step >= ahead)
        def _():
            for copy in weight_copies(step):
                copy.wait()

        def two(i, carry):
            multiply(step, 2 * i, 2)
            return carry

        lax.fori_loop(0, lax.div(count, 2), two, 0)

        @pl.when(lax.rem(count, 2) == 1)
        def _():
            multiply(step, count - 1, 1)

        @pl.when(step + depth < steps)
        def _():
            for copy in weight_copies(step + depth):
                copy.start()

        @pl.when(step + depth == steps)
        def _():
            if after_width:
                for copy in weight_copies(steps):
                    copy.start()

        return carry

    @pl.when(count > 0)
    def _():
        if prepare:

            def start_rows(place, carry):
                for copy in row_copies(place):
                    copy.start()
                return carry

            lax.fori_loop(0, count, start_rows, 0)
        for step in range(ahead, 1 if prepare else min(depth, wanted)):
            for copy in weight_copies(step):
                copy.start()

    for mask in range(blocks):

        @pl.when(layout[0, block_of(mask)] != mine)
        def _(mask=mask):
            for side in range(2):
                slot = slot_of(mask, side)
                cols = pl.ds(side * (width // 2), width // 2)
                zeros = jnp.zeros((HALF, width // 2), jnp.bfloat16)
                keep[slot, :, cols] = zeros
                for low, high, send in sends:
                    if low <= slot < high:
                        send[slot - low, :, cols] = zeros

    @pl.when(count > 0)
    def _():
        if prepare:
            lax.fori_loop(0, count, prepare_block, 0)
            for step in range(1, min(depth, wanted)):
                for copy in weight_copies(step):
                    copy.start()
        lax.fori_loop(0, steps, one_tile, 0)
        for step in range(steps, wanted):
            for copy in weight_copies(step):
                copy.wait()


def terms(layout, rows, w_gate, w_up, first, width, after_width, xor, waits=()):
    prepare = len(rows) == 3
    blocks = layout.shape[1]
    hid, columns = w_gate.shape
    tile = columns // sum(PLAN)
    parts = [(0, blocks)] + parts_of(blocks, xor)
    hbm_spec = pl.BlockSpec(memory_space=HBM)
    vmem_spec = pl.BlockSpec(memory_space=VMEM)
    out_shape = [pltpu.VMEM((DEPTH, 2 * hid, tile), jnp.bfloat16)]
    out_shape += [jax.ShapeDtypeStruct((b - a, HALF, width), jnp.bfloat16) for a, b in parts]
    scratch = [pltpu.SMEM((blocks,), jnp.int32), pltpu.SemaphoreType.DMA((DEPTH, 4))]
    if prepare:
        out_shape.append(pltpu.VMEM((blocks * BLOCK, 2 * hid), jnp.bfloat16))
        scratch.append(pltpu.VMEM((blocks, 3, BLOCK, hid), jnp.bfloat16))
        scratch.append(pltpu.SemaphoreType.DMA((blocks, 3)))
    constrain = pltpu.with_memory_space_constraint
    rows = [constrain(r, HBM if prepare else VMEM) for r in rows]
    return pl.pallas_call(
        functools.partial(
            terms_kernel,
            first=first,
            after_width=after_width,
            prepare=prepare,
            waits=len(waits),
            xor=xor,
        ),
        in_specs=[pl.BlockSpec(memory_space=pltpu.MemorySpace.SMEM)]
        + ([hbm_spec] * 3 if prepare else [vmem_spec] * 2)
        + [hbm_spec] * 2
        + [pl.BlockSpec(memory_space=pl.ANY)] * len(waits),
        out_specs=[vmem_spec] * len(out_shape),
        out_shape=out_shape,
        scratch_shapes=scratch,
        input_output_aliases={} if prepare else {2: 0},
        compiler_params=pltpu.CompilerParams(vmem_limit_bytes=24 * 2**20),
        cost_estimate=pl.CostEstimate(
            flops=2 * blocks * BLOCK * 2 * hid * width,
            bytes_accessed=4 * hid * width,
            transcendentals=0,
        ),
        name="terms",
    )(layout, *rows, constrain(w_gate, HBM), constrain(w_up, HBM), *waits)


def swapped(x, axis, mask):
    return lax.ppermute(x, axis, [(i, i ^ mask) for i in range(lax.axis_size(axis))])


def passed_along(x, axis, by):
    size = lax.axis_size(axis)
    return lax.ppermute(x, axis, [(i, (i + by) % size) for i in range(size)])


def chunk_widths(width):
    unit = width // sum(PLAN)
    return [unit * n for n in PLAN]


def wide(x):
    return x.astype(jnp.float32)


def narrow(x):
    return x.astype(jnp.bfloat16)


def after(x, arrays):
    for a in arrays:
        a = a.reshape((-1,) + a.shape[-2:])[0, : x.shape[-2], : x.shape[-1]]
        short = [(0, n - m) for n, m in zip(x.shape[-2:], a.shape)]
        x = x + 0 * jnp.pad(a, short)
    return x


class Chunk:
    def __init__(self, keep, sends, xor, waits):
        self.keep, self.xor = keep, xor
        half = keep.shape[-1] // 2
        self.sides = [(slice(0, half), 2), (slice(half, None), 1)]
        self.other = []
        for i, send in enumerate(sends):
            other = swapped(after(send, waits) if i == 1 else send, "tensor", 1)
            self.other += [other[i] for i in range(other.shape[0])]

    def pair(self, slot, cols=slice(None)):
        return wide(self.keep[slot, :, cols]) + wide(self.other[slot][:, cols])

    def first_half(self):
        if self.xor:
            self.far = [
                narrow(jnp.stack([self.pair(2, cols), self.pair(3, cols)])) for cols, _ in self.sides
            ]
            self.near = [swapped(far, "dp", bit) for far, (_, bit) in zip(self.far, self.sides)]
        else:
            slots = [self.pair(slot) for slot in range(len(self.other))]
            self.far, self.near = [narrow(jnp.stack(slots))], []

    def second_half(self, waits):
        if self.xor:
            self.last = []
            for near, (cols, bit) in zip(self.near, self.sides):
                far = after(self.pair(1, cols) + wide(near[1]), [wide(a) for a in waits])
                self.last.append(swapped(narrow(far), "dp", 3 - bit))
        else:
            self.last = [lax.psum_scatter(self.far[0], "dp", scatter_dimension=0, tiled=True)[0]]

    def finish(self, waits):
        if self.xor:
            out = [
                self.pair(0, cols) + wide(near[0]) + wide(last)
                for near, last, (cols, _) in zip(self.near, self.last, self.sides)
            ]
            self.sum = jnp.concatenate([narrow(after(o, [wide(a) for a in waits])) for o in out], axis=1)
        else:
            self.sum = self.last[0]
        self.out = passed_along(self.sum, "section", -1)


def per_device(grad_hidden, gate_pre, up_pre, w_gate, w_up, block_expert):
    xor = lax.axis_size("dp") == 4
    widths = chunk_widths(w_gate.shape[2])
    rows = [grad_hidden[0], gate_pre[0], up_pre[0]]
    chunks, waits = [], []
    first = 0
    for c, (width, after_width) in enumerate(zip(widths, widths[1:] + [0])):
        ring, keep, *rest = terms(
            block_expert, rows, w_gate[0], w_up[0], first, width, after_width, xor, waits
        )
        first += width
        parts = len(parts_of(keep.shape[0], xor))
        packed = rest[parts] if c == 0 else rows[0]
        rows = [packed, ring]
        ready = [chunks[c - 3].out] if c >= 3 else []
        ready += chunks[c - 2].last if c >= 2 else []
        ready += chunks[c - 1].near if c >= 1 and after_width else []
        chunks.append(Chunk(keep, rest[:parts], xor, ready))
        chunks[c].first_half()
        if c >= 1:
            chunks[c - 1].second_half([keep])
        if c >= 2:
            chunks[c - 2].finish([keep])
        waits = chunks[c].far + ([chunks[c - 2].sum] if c >= 2 else [])
    chunks[-1].second_half([])
    chunks[-2].finish(chunks[-1].far[:1])
    chunks[-1].finish([chunks[-3].out])
    return jnp.concatenate([chunk.out for chunk in chunks], axis=1)[None]


def solution(mesh):
    return jax.shard_map(
        per_device,
        mesh=mesh,
        in_specs=(
            P("section", None, ("dp", "tensor")),
            P("section", None, ("dp", "tensor")),
            P("section", None, ("dp", "tensor")),
            P("section", ("dp", "tensor"), None),
            P("section", ("dp", "tensor"), None),
            P("section", None),
        ),
        out_specs=P("section", ("dp", "tensor"), None),
        check_vma=False,
    )
```

profile of v0, /device:TPU:0, one launch (start us, length us, event | category | flops | bytes accessed | tf_op | source)
XLA Modules:
  0.0 79.5 jit_solution(2340244699218079859)
XLA Ops:
  0.0 0.7 copy-done
  0.7 8.4 %terms.4 = (bf16[3,4096,512]{2,1,0:T(8,128)(2,1)S(1)}, bf16[4,64,1536]{2,1,0:T(8,128)(2,1)S(1)}, bf16[2,64,1536]{2,1,0:T(8,128)(2,1)S(1)}, bf16[1,64,1536]{2,1,0...) custom-call(s32[1,4]{1,0:T(1,128)S(1)} %copy-done, bf16[512,2048]{1,0:T(8,128)(2,1)} %bitcast.298, ...), custom_call_target="tpu_custom_call" | custom-call | flops 6442450944 | bytes 12582912 | tf_op jit(solution)/shard_map/terms/pallas_call | solution.py:223
  9.1 0.5 collective-permute-start.1
  9.6 0.1 collective-permute-start.2
  9.7 0.4 collective-permute-start
  10.1 0.6 collective-permute-done.1
  10.7 0.4 collective-permute-done.2
  11.0 0.1 fusion.71
  11.2 2.9 %collective-permute-start.3 = (bf16[2,64,768]{2,1,0:T(8,128)(2,1)S(1)}, bf16[2,64,768]{2,1,0:T(8,128)(2,1)S(1)}, u32[]{:S(2)}, u32[]{:S(2)}) collective-permute-start(bf16[2,64,768]{2,1,0:T(8,128)(2,1)S(1)} %pad_maximum_fusion.3.refs_5_), channel_id=1, source_target_pairs={{0,4},{2,6},{4,0},{6,2},{1,5},{3,7},{5,1},{7,3},{8,12},{10,14},{12... | collective-permute-start | bytes 589832 | tf_op jit(solution)/shard_map/ppermute | solution.py:251
  14.0 1.6 %collective-permute-start.5 = (bf16[2,64,768]{2,1,0:T(8,128)(2,1)S(1)}, bf16[2,64,768]{2,1,0:T(8,128)(2,1)S(1)}, u32[]{:S(2)}, u32[]{:S(2)}) collective-permute-start(bf16[2,64,768]{2,1,0:T(8,128)(2,1)S(1)} %pad_maximum_fusion.4.refs_6_), channel_id=1, source_target_pairs={{0,2},{2,0},{4,6},{6,4},{1,3},{3,1},{5,7},{7,5},{8,10},{10,8},{12,... | collective-permute-start | bytes 589832 | tf_op jit(solution)/shard_map/ppermute | solution.py:251
  15.6 7.0 %terms.5 = (bf16[3,4096,512]{2,1,0:T(8,128)(2,1)S(1)}, bf16[4,64,2048]{2,1,0:T(8,128)(2,1)S(1)}, bf16[2,64,2048]{2,1,0:T(8,128)(2,1)S(1)}, bf16[1,64,2048]{2,1,0:T(8,128)(2,1)S(1)}, bf16[1,64,2048]{2,1,0:T(8,128)(2,1)S(1)}) custom-call(s32[1,4]{1,0:T(1,128)S(1)} %copy-done, ...), custom_call_target="tpu_custom_call", output_to_operand_aliasing={{0}: (2, {})} | custom-call | flops 8589934592 | bytes 16777216 | tf_op jit(solution)/shard_map/terms/pallas_call | solution.py:223
  22.6 0.1 collective-permute-start.7
  22.7 0.5 collective-permute-start.10
  23.2 0.0 collective-permute-done.3
  23.2 0.1 bitcast_add_fusion
  23.3 0.1 collective-permute-start.6
  23.5 0.1 fusion.43
  23.6 0.6 collective-permute-start.4
  24.2 0.0 collective-permute-start.8
  24.2 1.1 %collective-permute-done.6 = bf16[1,64,2048]{2,1,0:T(8,128)(2,1)S(1)} collective-permute-done((bf16[1,64,2048]{2,1,0:T(8,128)(2,1)S(1)}, bf16[1,64,2048]{2,1,0:T(8,128)(2,1)S(1)}, u32[]{:S(2)}, u32[]{:S(2)}) %collective-permute-start.6) | collective-permute-done | bytes 262176 | tf_op jit(solution)/shard_map/ppermute | solution.py:251
  25.4 0.2 fusion.52
  25.6 0.9 %collective-permute-start.11 = (bf16[2,64,1024]{2,1,0:T(8,128)(2,1)S(1)}, bf16[2,64,1024]{2,1,0:T(8,128)(2,1)S(1)}, u32[]{:S(2)}, u32[]{:S(2)}) collective-permute-start(bf16[2,64,1024]{2,1,0:T(8,128)(2,1)S(1)} %pad_maximum_fusion.refs_5_), channel_id=1, source_target_pairs={{0,4},{2,6},{4,0},{6,2},{1,5},{3,7},{5,1},{7,3},{8,12},{10,14},{12... | collective-permute-start | bytes 786440 | tf_op jit(solution)/shard_map/ppermute | solution.py:251
  26.6 1.5 %collective-permute-start.13 = (bf16[2,64,1024]{2,1,0:T(8,128)(2,1)S(1)}, bf16[2,64,1024]{2,1,0:T(8,128)(2,1)S(1)}, u32[]{:S(2)}, u32[]{:S(2)}) collective-permute-start(bf16[2,64,1024]{2,1,0:T(8,128)(2,1)S(1)} %pad_maximum_fusion.1.refs_6_), channel_id=1, source_target_pairs={{0,2},{2,0},{4,6},{6,4},{1,3},{3,1},{5,7},{7,5},{8,10},{10,8},{12,... | collective-permute-start | bytes 786440 | tf_op jit(solution)/shard_map/ppermute | solution.py:251
  28.1 5.7 %terms.6 = (bf16[3,4096,512]{2,1,0:T(8,128)(2,1)S(1)}, bf16[4,64,1536]{2,1,0:T(8,128)(2,1)S(1)}, bf16[2,64,1536]{2,1,0:T(8,128)(2,1)S(1)}, bf16[1,64,1536]{2,1,0:T(8,128)(2,1)S(1)}, bf16[1,64,1536]{2,1,0:T(8,128)(2,1)S(1)}) custom-call(s32[1,4]{1,0:T(1,128)S(1)} %copy-done, ...), custom_call_target="tpu_custom_call", output_to_operand_aliasing={{0}: (2, {})} | custom-call | flops 6442450944 | bytes 12582912 | tf_op jit(solution)/shard_map/terms/pallas_call | solution.py:223
  33.8 0.2 convert_element_type.517
  34.0 0.1 collective-permute-start.15
  34.1 0.5 collective-permute-start.18
  34.5 0.1 fusion.49
  34.7 14.5 %collective-permute-start.9 = (bf16[64,1536]{1,0:T(8,128)(2,1)S(1)}, bf16[64,1536]{1,0:T(8,128)(2,1)S(1)}, u32[]{:S(2)}, u32[]{:S(2)}) collective-permute-start(bf16[64,1536]{1,0:T(8,128)(2,1)S(1)} %pad_maximum_fusion.5.refs_7_), channel_id=1, source_target_pairs={{0,24},{8,0},{16,8},{24,16},{1,25},{9,1},{17,9},{25,17},{2,26},{10... | collective-permute-start | bytes 589832 | tf_op jit(solution)/shard_map/ppermute | solution.py:256
  49.3 0.1 bitcast_add_fusion.2
  49.5 0.1 collective-permute-start.14
  49.5 0.1 fusion.9
  49.7 0.6 collective-permute-start.12
  50.3 0.6 collective-permute-done.14
  51.0 0.1 fusion.75
  51.1 1.5 %collective-permute-start.19 = (bf16[2,64,768]{2,1,0:T(8,128)(2,1)S(1)}, bf16[2,64,768]{2,1,0:T(8,128)(2,1)S(1)}, u32[]{:S(2)}, u32[]{:S(2)}) collective-permute-start(bf16[2,64,768]{2,1,0:T(8,128)(2,1)S(1)} %pad_maximum_fusion.6.refs_5_), channel_id=1, source_target_pairs={{0,4},{2,6},{4,0},{6,2},{1,5},{3,7},{5,1},{7,3},{8,12},{10,14},{12... | collective-permute-start | bytes 589832 | tf_op jit(solution)/shard_map/ppermute | solution.py:251
  52.6 1.6 %collective-permute-start.22 = (bf16[2,64,768]{2,1,0:T(8,128)(2,1)S(1)}, bf16[2,64,768]{2,1,0:T(8,128)(2,1)S(1)}, u32[]{:S(2)}, u32[]{:S(2)}) collective-permute-start(bf16[2,64,768]{2,1,0:T(8,128)(2,1)S(1)} %pad_maximum_fusion.7.refs_6_), channel_id=1, source_target_pairs={{0,2},{2,0},{4,6},{6,4},{1,3},{3,1},{5,7},{7,5},{8,10},{10,8},{12,... | collective-permute-start | bytes 589832 | tf_op jit(solution)/shard_map/ppermute | solution.py:251
  54.1 4.2 %terms.7 = (bf16[3,4096,512]{2,1,0:T(8,128)(2,1)S(1)}, bf16[4,64,1024]{2,1,0:T(8,128)(2,1)S(1)}, bf16[2,64,1024]{2,1,0:T(8,128)(2,1)S(1)}, bf16[1,64,1024]{2,1,0:T(8,128)(2,1)S(1)}, bf16[1,64,1024]{2,1,0:T(8,128)(2,1)S(1)}) custom-call(s32[1,4]{1,0:T(1,128)S(1)} %copy-done, ...), custom_call_target="tpu_custom_call", output_to_operand_aliasing={{0}: (2, {})} | custom-call | flops 4294967296 | bytes 8388608 | tf_op jit(solution)/shard_map/terms/pallas_call | solution.py:223
  58.4 0.1 collective-permute-start.26
  58.5 0.5 collective-permute-start.21
  59.1 0.1 collective-permute-start.25
  59.2 0.1 convert_element_type.554
  59.3 0.2 fusion.13
  59.5 0.3 collective-permute-done.26
  59.8 2.0 %collective-permute-start.17 = (bf16[64,2048]{1,0:T(8,128)(2,1)S(1)}, bf16[64,2048]{1,0:T(8,128)(2,1)S(1)}, u32[]{:S(2)}, u32[]{:S(2)}) collective-permute-start(bf16[64,2048]{1,0:T(8,128)(2,1)S(1)} %pad_maximum_fusion.2), channel_id=1, source_target_pairs={{0,24},{8,0},{16,8},{24,16},{1,25},{9,1},{17,9},{25,17},{2,26},{10... | collective-permute-start | bytes 786440 | tf_op jit(solution)/shard_map/ppermute | solution.py:256
  61.8 0.1 fusion.68
  61.9 0.1 collective-permute-start.27
  62.0 0.7 collective-permute-start.29
  62.7 0.1 fusion.26
  62.8 1.4 %collective-permute-start.20 = (bf16[64,768]{1,0:T(8,128)(2,1)S(1)}, bf16[64,768]{1,0:T(8,128)(2,1)S(1)}, u32[]{:S(2)}, u32[]{:S(2)}) collective-permute-start(bf16[64,768]{1,0:T(8,128)(2,1)S(1)} %get-tuple-element.51), channel_id=1, source_target_pairs={{0,2},{2,0},{4,6},{6,4},{1,3},{3,1},{5,7},{7,5},{8,10},{10,8},{12,... | collective-permute-start | bytes 294920 | tf_op jit(solution)/shard_map/ppermute | solution.py:251
  64.2 2.0 %collective-permute-start.23 = (bf16[64,768]{1,0:T(8,128)(2,1)S(1)}, bf16[64,768]{1,0:T(8,128)(2,1)S(1)}, u32[]{:S(2)}, u32[]{:S(2)}) collective-permute-start(bf16[64,768]{1,0:T(8,128)(2,1)S(1)} %get-tuple-element.52), channel_id=1, source_target_pairs={{0,4},{2,6},{4,0},{6,2},{1,5},{3,7},{5,1},{7,3},{8,12},{10,14},{12... | collective-permute-start | bytes 294920 | tf_op jit(solution)/shard_map/ppermute | solution.py:251
  66.3 2.0 %collective-permute-done.27 = bf16[2,64,512]{2,1,0:T(8,128)(2,1)S(1)} collective-permute-done((bf16[2,64,512]{2,1,0:T(8,128)(2,1)S(1)}, bf16[2,64,512]{2,1,0:T(8,128)(2,1)S(1)}, u32[]{:S(2)}, u32[]{:S(2)}) %collective-permute-start.27) | collective-permute-done | bytes 131104 | tf_op jit(solution)/shard_map/ppermute | solution.py:251
  68.3 0.1 collective-permute-done.29
  68.4 0.1 fusion.63
  68.5 0.7 collective-permute-start.28
  69.2 1.7 %collective-permute-start.30 = (bf16[64,512]{1,0:T(8,128)(2,1)S(1)}, bf16[64,512]{1,0:T(8,128)(2,1)S(1)}, u32[]{:S(2)}, u32[]{:S(2)}) collective-permute-start(bf16[64,512]{1,0:T(8,128)(2,1)S(1)} %get-tuple-element.78), channel_id=1, source_target_pairs={{0,4},{2,6},{4,0},{6,2},{1,5},{3,7},{5,1},{7,3},{8,12},{10,14},{12... | collective-permute-start | bytes 196616 | tf_op jit(solution)/shard_map/ppermute | solution.py:251
  70.9 0.1 fusion.29
  71.1 0.6 collective-permute-start.24
  71.7 1.1 %collective-permute-done.28 = bf16[64,512]{1,0:T(8,128)(2,1)S(1)} collective-permute-done((bf16[64,512]{1,0:T(8,128)(2,1)S(1)}, bf16[64,512]{1,0:T(8,128)(2,1)S(1)}, u32[]{:S(2)}, u32[]{:S(2)}) %collective-permute-start.28) | collective-permute-done | bytes 65568 | tf_op jit(solution)/shard_map/ppermute | solution.py:251
  72.8 0.7 collective-permute-done.30
  73.5 0.1 fusion.66
  73.6 0.3 collective-permute-start.31
  73.9 4.7 %collective-permute-done.31 = bf16[64,1024]{1,0:T(8,128)(2,1)S(1)} collective-permute-done((bf16[64,1024]{1,0:T(8,128)(2,1)S(1)}, bf16[64,1024]{1,0:T(8,128)(2,1)S(1)}, u32[]{:S(2)}, u32[]{:S(2)}) %collective-permute-start.31) | collective-permute-done | bytes 131104 | tf_op jit(solution)/shard_map/ppermute | solution.py:256
  78.6 0.9 %maximum_bitcast_fusion = bf16[1,64,6144]{2,1,0:T(8,128)(2,1)} fusion(bf16[64,1024]{1,0:T(8,128)(2,1)S(1)} %collective-permute-done.31, bf16[64,1536]{1,0:T(8,128)(2,1)S(1)} %collective-permute-done.24, bf16[64,2048]{1,0:T(8,128)(2,1)S(1)} %collective-permute-done.17, bf16[64,1536]{1,0:T(8,128)(2,1)S(1)} %collective-permute-done.9), kind=kLoop, calls=%fused_computation | loop fusion | flops 3145728 | bytes 1572864 | tf_op jit(solution)/shard_map/broadcast_in_dim | solution.py:351
  (44 shorter events, 0.5 us)
Async XLA Ops:
  0.0 0.7 copy-start
  9.1 1.6 %collective-permute-start.1 = (bf16[1,64,1536]{2,1,0:T(8,128)(2,1)S(1)}, bf16[1,64,1536]{2,1,0:T(8,128)(2,1)S(1)}, u32[]{:S(2)}, u32[]{:S(2)}) collective-permute-start(bf16[1,64,1536]{2,1,0:T(8,128)(2,1)S(1)} %get-tuple-element.27), channel_id=1, source_target_pairs={{0,1},{1,0},{2,3},{3,2},{4,5},{5,4},{6,7},{7,6},{8,9},{9,8},{10,11... | collective-permute-start | bytes 589832 | tf_op jit(solution)/shard_map/ppermute | solution.py:251
  9.6 1.4 %collective-permute-start.2 = (bf16[1,64,1536]{2,1,0:T(8,128)(2,1)S(1)}, bf16[1,64,1536]{2,1,0:T(8,128)(2,1)S(1)}, u32[]{:S(2)}, u32[]{:S(2)}) collective-permute-start(bf16[1,64,1536]{2,1,0:T(8,128)(2,1)S(1)} %get-tuple-element.28), channel_id=1, source_target_pairs={{0,1},{1,0},{2,3},{3,2},{4,5},{5,4},{6,7},{7,6},{8,9},{9,8},{10,11... | collective-permute-start | bytes 589832 | tf_op jit(solution)/shard_map/ppermute | solution.py:251
  9.7 13.8 %collective-permute-start = (bf16[2,64,1536]{2,1,0:T(8,128)(2,1)S(1)}, bf16[2,64,1536]{2,1,0:T(8,128)(2,1)S(1)}, u32[]{:S(2)}, u32[]{:S(2)}) collective-permute-start(bf16[2,64,1536]{2,1,0:T(8,128)(2,1)S(1)} %get-tuple-element.26), channel_id=1, source_target_pairs={{0,1},{1,0},{2,3},{3,2},{4,5},{5,4},{6,7},{7,6},{8,9},{9,8},{10,11... | collective-permute-start | bytes 1179656 | tf_op jit(solution)/shard_map/ppermute | solution.py:251
  11.2 12.1 %collective-permute-start.3 = (bf16[2,64,768]{2,1,0:T(8,128)(2,1)S(1)}, bf16[2,64,768]{2,1,0:T(8,128)(2,1)S(1)}, u32[]{:S(2)}, u32[]{:S(2)}) collective-permute-start(bf16[2,64,768]{2,1,0:T(8,128)(2,1)S(1)} %pad_maximum_fusion.3.refs_5_), channel_id=1, source_target_pairs={{0,4},{2,6},{4,0},{6,2},{1,5},{3,7},{5,1},{7,3},{8,12},{10,14},{12... | collective-permute-start | bytes 589832 | tf_op jit(solution)/shard_map/ppermute | solution.py:251
  14.0 9.2 %collective-permute-start.5 = (bf16[2,64,768]{2,1,0:T(8,128)(2,1)S(1)}, bf16[2,64,768]{2,1,0:T(8,128)(2,1)S(1)}, u32[]{:S(2)}, u32[]{:S(2)}) collective-permute-start(bf16[2,64,768]{2,1,0:T(8,128)(2,1)S(1)} %pad_maximum_fusion.4.refs_6_), channel_id=1, source_target_pairs={{0,2},{2,0},{4,6},{6,4},{1,3},{3,1},{5,7},{7,5},{8,10},{10,8},{12,... | collective-permute-start | bytes 589832 | tf_op jit(solution)/shard_map/ppermute | solution.py:251
  22.6 1.6 %collective-permute-start.7 = (bf16[1,64,2048]{2,1,0:T(8,128)(2,1)S(1)}, bf16[1,64,2048]{2,1,0:T(8,128)(2,1)S(1)}, u32[]{:S(2)}, u32[]{:S(2)}) collective-permute-start(bf16[1,64,2048]{2,1,0:T(8,128)(2,1)S(1)} %get-tuple-element.34), channel_id=1, source_target_pairs={{0,1},{1,0},{2,3},{3,2},{4,5},{5,4},{6,7},{7,6},{8,9},{9,8},{10,11... | collective-permute-start | bytes 786440 | tf_op jit(solution)/shard_map/ppermute | solution.py:251
  22.7 12.0 %collective-permute-start.10 = (bf16[2,64,2048]{2,1,0:T(8,128)(2,1)S(1)}, bf16[2,64,2048]{2,1,0:T(8,128)(2,1)S(1)}, u32[]{:S(2)}, u32[]{:S(2)}) collective-permute-start(bf16[2,64,2048]{2,1,0:T(8,128)(2,1)S(1)} %get-tuple-element.36), channel_id=1, source_target_pairs={{0,1},{1,0},{2,3},{3,2},{4,5},{5,4},{6,7},{7,6},{8,9},{9,8},{10,11... | collective-permute-start | bytes 1572872 | tf_op jit(solution)/shard_map/ppermute | solution.py:251
  23.3 2.0 %collective-permute-start.6 = (bf16[1,64,2048]{2,1,0:T(8,128)(2,1)S(1)}, bf16[1,64,2048]{2,1,0:T(8,128)(2,1)S(1)}, u32[]{:S(2)}, u32[]{:S(2)}) collective-permute-start(bf16[1,64,2048]{2,1,0:T(8,128)(2,1)S(1)} %bitcast_add_fusion), channel_id=1, source_target_pairs={{0,1},{1,0},{2,3},{3,2},{4,5},{5,4},{6,7},{7,6},{8,9},{9,8},{10,11... | collective-permute-start | bytes 786440 | tf_op jit(solution)/shard_map/ppermute | solution.py:251
  23.6 10.4 %collective-permute-start.4 = (bf16[64,768]{1,0:T(8,128)(2,1)S(1)}, bf16[64,768]{1,0:T(8,128)(2,1)S(1)}, u32[]{:S(2)}, u32[]{:S(2)}) collective-permute-start(bf16[64,768]{1,0:T(8,128)(2,1)S(1)} %get-tuple-element.53), channel_id=1, source_target_pairs={{0,2},{2,0},{4,6},{6,4},{1,3},{3,1},{5,7},{7,5},{8,10},{10,8},{12,... | collective-permute-start | bytes 294920 | tf_op jit(solution)/shard_map/ppermute | solution.py:251
  24.2 9.8 %collective-permute-start.8 = (bf16[64,768]{1,0:T(8,128)(2,1)S(1)}, bf16[64,768]{1,0:T(8,128)(2,1)S(1)}, u32[]{:S(2)}, u32[]{:S(2)}) collective-permute-start(bf16[64,768]{1,0:T(8,128)(2,1)S(1)} %get-tuple-element.54), channel_id=1, source_target_pairs={{0,4},{2,6},{4,0},{6,2},{1,5},{3,7},{5,1},{7,3},{8,12},{10,14},{12... | collective-permute-start | bytes 294920 | tf_op jit(solution)/shard_map/ppermute | solution.py:251
  25.6 23.7 %collective-permute-start.11 = (bf16[2,64,1024]{2,1,0:T(8,128)(2,1)S(1)}, bf16[2,64,1024]{2,1,0:T(8,128)(2,1)S(1)}, u32[]{:S(2)}, u32[]{:S(2)}) collective-permute-start(bf16[2,64,1024]{2,1,0:T(8,128)(2,1)S(1)} %pad_maximum_fusion.refs_5_), channel_id=1, source_target_pairs={{0,4},{2,6},{4,0},{6,2},{1,5},{3,7},{5,1},{7,3},{8,12},{10,14},{12... | collective-permute-start | bytes 786440 | tf_op jit(solution)/shard_map/ppermute | solution.py:251
  26.6 22.8 %collective-permute-start.13 = (bf16[2,64,1024]{2,1,0:T(8,128)(2,1)S(1)}, bf16[2,64,1024]{2,1,0:T(8,128)(2,1)S(1)}, u32[]{:S(2)}, u32[]{:S(2)}) collective-permute-start(bf16[2,64,1024]{2,1,0:T(8,128)(2,1)S(1)} %pad_maximum_fusion.1.refs_6_), channel_id=1, source_target_pairs={{0,2},{2,0},{4,6},{6,4},{1,3},{3,1},{5,7},{7,5},{8,10},{10,8},{12,... | collective-permute-start | bytes 786440 | tf_op jit(solution)/shard_map/ppermute | solution.py:251
  34.0 16.4 %collective-permute-start.15 = (bf16[1,64,1536]{2,1,0:T(8,128)(2,1)S(1)}, bf16[1,64,1536]{2,1,0:T(8,128)(2,1)S(1)}, u32[]{:S(2)}, u32[]{:S(2)}) collective-permute-start(bf16[1,64,1536]{2,1,0:T(8,128)(2,1)S(1)} %get-tuple-element.39), channel_id=1, source_target_pairs={{0,1},{1,0},{2,3},{3,2},{4,5},{5,4},{6,7},{7,6},{8,9},{9,8},{10,11... | collective-permute-start | bytes 589832 | tf_op jit(solution)/shard_map/ppermute | solution.py:251
  34.1 16.2 %collective-permute-start.18 = (bf16[2,64,1536]{2,1,0:T(8,128)(2,1)S(1)}, bf16[2,64,1536]{2,1,0:T(8,128)(2,1)S(1)}, u32[]{:S(2)}, u32[]{:S(2)}) collective-permute-start(bf16[2,64,1536]{2,1,0:T(8,128)(2,1)S(1)} %get-tuple-element.41), channel_id=1, source_target_pairs={{0,1},{1,0},{2,3},{3,2},{4,5},{5,4},{6,7},{7,6},{8,9},{9,8},{10,11... | collective-permute-start | bytes 1179656 | tf_op jit(solution)/shard_map/ppermute | solution.py:251
  34.7 23.7 %collective-permute-start.9 = (bf16[64,1536]{1,0:T(8,128)(2,1)S(1)}, bf16[64,1536]{1,0:T(8,128)(2,1)S(1)}, u32[]{:S(2)}, u32[]{:S(2)}) collective-permute-start(bf16[64,1536]{1,0:T(8,128)(2,1)S(1)} %pad_maximum_fusion.5.refs_7_), channel_id=1, source_target_pairs={{0,24},{8,0},{16,8},{24,16},{1,25},{9,1},{17,9},{25,17},{2,26},{10... | collective-permute-start | bytes 589832 | tf_op jit(solution)/shard_map/ppermute | solution.py:256
  49.5 1.5 %collective-permute-start.14 = (bf16[1,64,1536]{2,1,0:T(8,128)(2,1)S(1)}, bf16[1,64,1536]{2,1,0:T(8,128)(2,1)S(1)}, u32[]{:S(2)}, u32[]{:S(2)}) collective-permute-start(bf16[1,64,1536]{2,1,0:T(8,128)(2,1)S(1)} %bitcast_add_fusion.2), channel_id=1, source_target_pairs={{0,1},{1,0},{2,3},{3,2},{4,5},{5,4},{6,7},{7,6},{8,9},{9,8},{10,11... | collective-permute-start | bytes 589832 | tf_op jit(solution)/shard_map/ppermute | solution.py:251
  49.7 8.8 %collective-permute-start.12 = (bf16[64,1024]{1,0:T(8,128)(2,1)S(1)}, bf16[64,1024]{1,0:T(8,128)(2,1)S(1)}, u32[]{:S(2)}, u32[]{:S(2)}) collective-permute-start(bf16[64,1024]{1,0:T(8,128)(2,1)S(1)} %get-tuple-element.45), channel_id=1, source_target_pairs={{0,2},{2,0},{4,6},{6,4},{1,3},{3,1},{5,7},{7,5},{8,10},{10,8},{12,... | collective-permute-start | bytes 393224 | tf_op jit(solution)/shard_map/ppermute | solution.py:251
  50.3 8.2 %collective-permute-start.16 = (bf16[64,1024]{1,0:T(8,128)(2,1)S(1)}, bf16[64,1024]{1,0:T(8,128)(2,1)S(1)}, u32[]{:S(2)}, u32[]{:S(2)}) collective-permute-start(bf16[64,1024]{1,0:T(8,128)(2,1)S(1)} %get-tuple-element.46), channel_id=1, source_target_pairs={{0,4},{2,6},{4,0},{6,2},{1,5},{3,7},{5,1},{7,3},{8,12},{10,14},{12... | collective-permute-start | bytes 393224 | tf_op jit(solution)/shard_map/ppermute | solution.py:251
  51.1 10.9 %collective-permute-start.19 = (bf16[2,64,768]{2,1,0:T(8,128)(2,1)S(1)}, bf16[2,64,768]{2,1,0:T(8,128)(2,1)S(1)}, u32[]{:S(2)}, u32[]{:S(2)}) collective-permute-start(bf16[2,64,768]{2,1,0:T(8,128)(2,1)S(1)} %pad_maximum_fusion.6.refs_5_), channel_id=1, source_target_pairs={{0,4},{2,6},{4,0},{6,2},{1,5},{3,7},{5,1},{7,3},{8,12},{10,14},{12... | collective-permute-start | bytes 589832 | tf_op jit(solution)/shard_map/ppermute | solution.py:251
  52.6 10.1 %collective-permute-start.22 = (bf16[2,64,768]{2,1,0:T(8,128)(2,1)S(1)}, bf16[2,64,768]{2,1,0:T(8,128)(2,1)S(1)}, u32[]{:S(2)}, u32[]{:S(2)}) collective-permute-start(bf16[2,64,768]{2,1,0:T(8,128)(2,1)S(1)} %pad_maximum_fusion.7.refs_6_), channel_id=1, source_target_pairs={{0,2},{2,0},{4,6},{6,4},{1,3},{3,1},{5,7},{7,5},{8,10},{10,8},{12,... | collective-permute-start | bytes 589832 | tf_op jit(solution)/shard_map/ppermute | solution.py:251
  58.4 1.4 %collective-permute-start.26 = (bf16[1,64,1024]{2,1,0:T(8,128)(2,1)S(1)}, bf16[1,64,1024]{2,1,0:T(8,128)(2,1)S(1)}, u32[]{:S(2)}, u32[]{:S(2)}) collective-permute-start(bf16[1,64,1024]{2,1,0:T(8,128)(2,1)S(1)} %get-tuple-element.44), channel_id=1, source_target_pairs={{0,1},{1,0},{2,3},{3,2},{4,5},{5,4},{6,7},{7,6},{8,9},{9,8},{10,11... | collective-permute-start | bytes 393224 | tf_op jit(solution)/shard_map/ppermute | solution.py:251
  58.5 3.2 %collective-permute-start.21 = (bf16[1,64,1024]{2,1,0:T(8,128)(2,1)S(1)}, bf16[1,64,1024]{2,1,0:T(8,128)(2,1)S(1)}, u32[]{:S(2)}, u32[]{:S(2)}) collective-permute-start(bf16[1,64,1024]{2,1,0:T(8,128)(2,1)S(1)} %fusion.56), channel_id=1, source_target_pairs={{0,1},{1,0},{2,3},{3,2},{4,5},{5,4},{6,7},{7,6},{8,9},{9,8},{10,11... | collective-permute-start | bytes 393224 | tf_op jit(solution)/shard_map/ppermute | solution.py:251
  59.1 5.2 %collective-permute-start.25 = (bf16[2,64,1024]{2,1,0:T(8,128)(2,1)S(1)}, bf16[2,64,1024]{2,1,0:T(8,128)(2,1)S(1)}, u32[]{:S(2)}, u32[]{:S(2)}) collective-permute-start(bf16[2,64,1024]{2,1,0:T(8,128)(2,1)S(1)} %get-tuple-element.43), channel_id=1, source_target_pairs={{0,1},{1,0},{2,3},{3,2},{4,5},{5,4},{6,7},{7,6},{8,9},{9,8},{10,11... | collective-permute-start | bytes 786440 | tf_op jit(solution)/shard_map/ppermute | solution.py:251
  59.8 11.9 %collective-permute-start.17 = (bf16[64,2048]{1,0:T(8,128)(2,1)S(1)}, bf16[64,2048]{1,0:T(8,128)(2,1)S(1)}, u32[]{:S(2)}, u32[]{:S(2)}) collective-permute-start(bf16[64,2048]{1,0:T(8,128)(2,1)S(1)} %pad_maximum_fusion.2), channel_id=1, source_target_pairs={{0,24},{8,0},{16,8},{24,16},{1,25},{9,1},{17,9},{25,17},{2,26},{10... | collective-permute-start | bytes 786440 | tf_op jit(solution)/shard_map/ppermute | solution.py:256
  61.9 6.4 %collective-permute-start.27 = (bf16[2,64,512]{2,1,0:T(8,128)(2,1)S(1)}, bf16[2,64,512]{2,1,0:T(8,128)(2,1)S(1)}, u32[]{:S(2)}, u32[]{:S(2)}) collective-permute-start(bf16[2,64,512]{2,1,0:T(8,128)(2,1)S(1)} %pad_maximum_fusion.9), channel_id=1, source_target_pairs={{0,4},{2,6},{4,0},{6,2},{1,5},{3,7},{5,1},{7,3},{8,12},{10,14},{12... | collective-permute-start | bytes 393224 | tf_op jit(solution)/shard_map/ppermute | solution.py:251
  62.0 6.4 %collective-permute-start.29 = (bf16[2,64,512]{2,1,0:T(8,128)(2,1)S(1)}, bf16[2,64,512]{2,1,0:T(8,128)(2,1)S(1)}, u32[]{:S(2)}, u32[]{:S(2)}) collective-permute-start(bf16[2,64,512]{2,1,0:T(8,128)(2,1)S(1)} %pad_maximum_fusion.10), channel_id=1, source_target_pairs={{0,2},{2,0},{4,6},{6,4},{1,3},{3,1},{5,7},{7,5},{8,10},{10,8},{12,... | collective-permute-start | bytes 393224 | tf_op jit(solution)/shard_map/ppermute | solution.py:251
  62.8 8.1 %collective-permute-start.20 = (bf16[64,768]{1,0:T(8,128)(2,1)S(1)}, bf16[64,768]{1,0:T(8,128)(2,1)S(1)}, u32[]{:S(2)}, u32[]{:S(2)}) collective-permute-start(bf16[64,768]{1,0:T(8,128)(2,1)S(1)} %get-tuple-element.51), channel_id=1, source_target_pairs={{0,2},{2,0},{4,6},{6,4},{1,3},{3,1},{5,7},{7,5},{8,10},{10,8},{12,... | collective-permute-start | bytes 294920 | tf_op jit(solution)/shard_map/ppermute | solution.py:251
  64.2 6.7 %collective-permute-start.23 = (bf16[64,768]{1,0:T(8,128)(2,1)S(1)}, bf16[64,768]{1,0:T(8,128)(2,1)S(1)}, u32[]{:S(2)}, u32[]{:S(2)}) collective-permute-start(bf16[64,768]{1,0:T(8,128)(2,1)S(1)} %get-tuple-element.52), channel_id=1, source_target_pairs={{0,4},{2,6},{4,0},{6,2},{1,5},{3,7},{5,1},{7,3},{8,12},{10,14},{12... | collective-permute-start | bytes 294920 | tf_op jit(solution)/shard_map/ppermute | solution.py:251
  68.5 4.3 %collective-permute-start.28 = (bf16[64,512]{1,0:T(8,128)(2,1)S(1)}, bf16[64,512]{1,0:T(8,128)(2,1)S(1)}, u32[]{:S(2)}, u32[]{:S(2)}) collective-permute-start(bf16[64,512]{1,0:T(8,128)(2,1)S(1)} %get-tuple-element.77), channel_id=1, source_target_pairs={{0,2},{2,0},{4,6},{6,4},{1,3},{3,1},{5,7},{7,5},{8,10},{10,8},{12,... | collective-permute-start | bytes 196616 | tf_op jit(solution)/shard_map/ppermute | solution.py:251
  69.2 4.3 %collective-permute-start.30 = (bf16[64,512]{1,0:T(8,128)(2,1)S(1)}, bf16[64,512]{1,0:T(8,128)(2,1)S(1)}, u32[]{:S(2)}, u32[]{:S(2)}) collective-permute-start(bf16[64,512]{1,0:T(8,128)(2,1)S(1)} %get-tuple-element.78), channel_id=1, source_target_pairs={{0,4},{2,6},{4,0},{6,2},{1,5},{3,7},{5,1},{7,3},{8,12},{10,14},{12... | collective-permute-start | bytes 196616 | tf_op jit(solution)/shard_map/ppermute | solution.py:251
  71.1 7.5 %collective-permute-start.24 = (bf16[64,1536]{1,0:T(8,128)(2,1)S(1)}, bf16[64,1536]{1,0:T(8,128)(2,1)S(1)}, u32[]{:S(2)}, u32[]{:S(2)}) collective-permute-start(bf16[64,1536]{1,0:T(8,128)(2,1)S(1)} %pad_maximum_fusion.8), channel_id=1, source_target_pairs={{0,24},{8,0},{16,8},{24,16},{1,25},{9,1},{17,9},{25,17},{2,26},{10... | collective-permute-start | bytes 589832 | tf_op jit(solution)/shard_map/ppermute | solution.py:256
  73.6 5.0 %collective-permute-start.31 = (bf16[64,1024]{1,0:T(8,128)(2,1)S(1)}, bf16[64,1024]{1,0:T(8,128)(2,1)S(1)}, u32[]{:S(2)}, u32[]{:S(2)}) collective-permute-start(bf16[64,1024]{1,0:T(8,128)(2,1)S(1)} %pad_maximum_fusion.11), channel_id=1, source_target_pairs={{0,24},{8,0},{16,8},{24,16},{1,25},{9,1},{17,9},{25,17},{2,26},{10... | collective-permute-start | bytes 393224 | tf_op jit(solution)/shard_map/ppermute | solution.py:256
where the time goes:
time: 78.3 us; the launch traced here: 79.5 us
  starting transfers between devices  38.3 us (49%)
  Pallas kernels  25.3 us (32%)
  waiting for transfers between devices  11.7 us (15%)
  other arithmetic  2.98 us (4%)
  local copies, waits for them, and re-layouts  0.8 us (1%)
    pallas_call x4, Pallas kernels, terms(): pl.pallas_call(functools.partial(terms_kernel, first=first, after_width=a...  25.3 us
    ppermute x28, starting transfers between devices, swapped(): lax.ppermute(x, axis, [(i, i ^ mask) for i in range(lax.axis_size(axis))])  21 us
    ppermute x4, starting transfers between devices, passed_along(): return lax.ppermute(x, axis, [(i, (i + by) % size) for i in range(size)])  17.4 us
    ppermute x28, waiting for transfers between devices, swapped(): lax.ppermute(x, axis, [(i, i ^ mask) for i in range(lax.axis_size(axis))])  6.95 us
    ppermute x4, waiting for transfers between devices, passed_along(): return lax.ppermute(x, axis, [(i, (i + by) % size) for i in range(size)])  4.73 us
  transfers between devices with their start and end apart: 32, of which 10 were waited for; matrix products, arithmetic and copies ran while one was open for 3% of the time, Pallas kernels for 21%

commit v1 on v0

--- a/solution.py
+++ b/solution.py
@@ -140,11 +140,15 @@
             for copy in weight_copies(step):
                 copy.wait()
 
-        def two(i, carry):
-            multiply(step, 2 * i, 2)
+        def four(i, carry):
+            multiply(step, 4 * i, 4)
             return carry
 
-        lax.fori_loop(0, lax.div(count, 2), two, 0)
+        lax.fori_loop(0, lax.div(count, 4), four, 0)
+
+        @pl.when(lax.rem(count, 4) >= 2)
+        def _():
+            multiply(step, lax.div(count, 4) * 4, 2)
 
         @pl.when(lax.rem(count, 2) == 1)
         def _():

time: 78.3 us -> 76.3 us (0.974)
  starting transfers between devices: 38.3 us -> 30.2 us
  Pallas kernels: 25.3 us -> 32.2 us
  waiting for transfers between devices: 11.7 us -> 10.4 us
    pallas_call x4, Pallas kernels: 25.3 us -> 32.2 us  [terms(): pl.pallas_call(functools.partial(terms_kernel, first=first, after_width=a...]
    ppermute x4, starting transfers between devices: 17.4 us -> 11.4 us  [passed_along(): return lax.ppermute(x, axis, [(i, (i + by) % size) for i in range(size)])]
    ppermute x28, starting transfers between devices: 21 us -> 18.8 us  [swapped(): lax.ppermute(x, axis, [(i, i ^ mask) for i in range(lax.axis_size(axis))])]
    ppermute x4, waiting for transfers between devices: 4.73 us -> 3.62 us  [passed_along(): return lax.ppermute(x, axis, [(i, (i + by) % size) for i in range(size)])]
  transfers between devices with their start and end apart: 32 -> 32, of which waited for: 10 -> 12; matrix products, arithmetic and copies ran while one was open for 3% -> 3% of each run, Pallas kernels for 21% -> 28%
where the time goes in v1:
time: 76.3 us; the launch traced here: 76.9 us
  Pallas kernels  32.2 us (42%)
  starting transfers between devices  30.2 us (40%)
  waiting for transfers between devices  10.4 us (14%)
  other arithmetic  2.98 us (4%)
  local copies, waits for them, and re-layouts  0.8 us (1%)
    pallas_call x4, Pallas kernels, terms(): pl.pallas_call(functools.partial(terms_kernel, first=first, after_width=a...  32.2 us
    ppermute x28, starting transfers between devices, swapped(): lax.ppermute(x, axis, [(i, i ^ mask) for i in range(lax.axis_size(axis))])  18.8 us
    ppermute x4, starting transfers between devices, passed_along(): return lax.ppermute(x, axis, [(i, (i + by) % size) for i in range(size)])  11.4 us
    ppermute x28, waiting for transfers between devices, swapped(): lax.ppermute(x, axis, [(i, i ^ mask) for i in range(lax.axis_size(axis))])  6.77 us
    ppermute x4, waiting for transfers between devices, passed_along(): return lax.ppermute(x, axis, [(i, (i + by) % size) for i in range(size)])  3.62 us
  transfers between devices with their start and end apart: 32, of which 12 were waited for; matrix products, arithmetic and copies ran while one was open for 3% of the time, Pallas kernels for 28%

profile of v1, /device:TPU:0, one launch (start us, length us, event | category | flops | bytes accessed | tf_op | source)
XLA Modules:
  0.0 76.9 jit_solution(6435834864204916062)
XLA Ops:
  0.0 0.7 copy-done
  0.7 10.8 %terms.4 = (bf16[3,4096,512]{2,1,0:T(8,128)(2,1)S(1)}, bf16[4,64,1536]{2,1,0:T(8,128)(2,1)S(1)}, bf16[2,64,1536]{2,1,0:T(8,128)(2,1)S(1)}, bf16[1,64,1536]{2,1,0...) custom-call(s32[1,4]{1,0:T(1,128)S(1)} %copy-done, bf16[512,2048]{1,0:T(8,128)(2,1)} %bitcast.298, ...), custom_call_target="tpu_custom_call" | custom-call | flops 6442450944 | bytes 12582912 | tf_op jit(solution)/shard_map/terms/pallas_call | solution.py:227
  11.4 0.5 collective-permute-start.1
  11.9 0.1 collective-permute-start.2
  12.0 0.4 collective-permute-start
  12.5 0.6 collective-permute-done.1
  13.0 0.4 collective-permute-done.2
  13.4 0.1 fusion.71
  13.5 0.1 collective-permute-start.3
  13.6 2.8 %collective-permute-start.5 = (bf16[2,64,768]{2,1,0:T(8,128)(2,1)S(1)}, bf16[2,64,768]{2,1,0:T(8,128)(2,1)S(1)}, u32[]{:S(2)}, u32[]{:S(2)}) collective-permute-start(bf16[2,64,768]{2,1,0:T(8,128)(2,1)S(1)} %pad_maximum_fusion.4.refs_6_), channel_id=1, source_target_pairs={{0,2},{2,0},{4,6},{6,4},{1,3},{3,1},{5,7},{7,5},{8,10},{10,8},{12,... | collective-permute-start | bytes 589832 | tf_op jit(solution)/shard_map/ppermute | solution.py:255
  16.5 9.3 %terms.5 = (bf16[3,4096,512]{2,1,0:T(8,128)(2,1)S(1)}, bf16[4,64,2048]{2,1,0:T(8,128)(2,1)S(1)}, bf16[2,64,2048]{2,1,0:T(8,128)(2,1)S(1)}, bf16[1,64,2048]{2,1,0:T(8,128)(2,1)S(1)}, bf16[1,64,2048]{2,1,0:T(8,128)(2,1)S(1)}) custom-call(s32[1,4]{1,0:T(1,128)S(1)} %copy-done, ...), custom_call_target="tpu_custom_call", output_to_operand_aliasing={{0}: (2, {})} | custom-call | flops 8589934592 | bytes 16777216 | tf_op jit(solution)/shard_map/terms/pallas_call | solution.py:227
  25.8 0.1 collective-permute-start.7
  25.8 0.5 collective-permute-start.10
  26.4 0.1 bitcast_add_fusion
  26.4 0.1 collective-permute-start.6
  26.6 0.1 fusion.43
  26.7 0.2 collective-permute-start.4
  27.0 0.4 collective-permute-done.7
  27.4 1.1 %collective-permute-done.6 = bf16[1,64,2048]{2,1,0:T(8,128)(2,1)S(1)} collective-permute-done((bf16[1,64,2048]{2,1,0:T(8,128)(2,1)S(1)}, bf16[1,64,2048]{2,1,0:T(8,128)(2,1)S(1)}, u32[]{:S(2)}, u32[]{:S(2)}) %collective-permute-start.6) | collective-permute-done | bytes 262176 | tf_op jit(solution)/shard_map/ppermute | solution.py:255
  28.5 0.2 fusion.52
  28.7 0.6 collective-permute-start.11
  29.3 1.9 %collective-permute-start.13 = (bf16[2,64,1024]{2,1,0:T(8,128)(2,1)S(1)}, bf16[2,64,1024]{2,1,0:T(8,128)(2,1)S(1)}, u32[]{:S(2)}, u32[]{:S(2)}) collective-permute-start(bf16[2,64,1024]{2,1,0:T(8,128)(2,1)S(1)} %pad_maximum_fusion.1.refs_6_), channel_id=1, source_target_pairs={{0,2},{2,0},{4,6},{6,4},{1,3},{3,1},{5,7},{7,5},{8,10},{10,8},{12,... | collective-permute-start | bytes 786440 | tf_op jit(solution)/shard_map/ppermute | solution.py:255
  31.2 7.1 %terms.6 = (bf16[3,4096,512]{2,1,0:T(8,128)(2,1)S(1)}, bf16[4,64,1536]{2,1,0:T(8,128)(2,1)S(1)}, bf16[2,64,1536]{2,1,0:T(8,128)(2,1)S(1)}, bf16[1,64,1536]{2,1,0:T(8,128)(2,1)S(1)}, bf16[1,64,1536]{2,1,0:T(8,128)(2,1)S(1)}) custom-call(s32[1,4]{1,0:T(1,128)S(1)} %copy-done, ...), custom_call_target="tpu_custom_call", output_to_operand_aliasing={{0}: (2, {})} | custom-call | flops 6442450944 | bytes 12582912 | tf_op jit(solution)/shard_map/terms/pallas_call | solution.py:227
  38.4 0.2 convert_element_type.517
  38.6 0.1 collective-permute-start.15
  38.7 0.5 collective-permute-start.18
  39.2 0.1 fusion.49
  39.3 0.2 collective-permute-start.9
  39.7 0.1 bitcast_add_fusion.2
  39.8 0.2 collective-permute-start.14
  39.9 0.1 fusion.9
  40.1 0.2 collective-permute-start.12
  40.3 0.3 collective-permute-done.18
  40.7 0.1 collective-permute-start.16
  40.8 0.5 collective-permute-done.14
  41.3 0.1 fusion.75
  41.4 1.5 %collective-permute-start.19 = (bf16[2,64,768]{2,1,0:T(8,128)(2,1)S(1)}, bf16[2,64,768]{2,1,0:T(8,128)(2,1)S(1)}, u32[]{:S(2)}, u32[]{:S(2)}) collective-permute-start(bf16[2,64,768]{2,1,0:T(8,128)(2,1)S(1)} %pad_maximum_fusion.6.refs_5_), channel_id=1, source_target_pairs={{0,4},{2,6},{4,0},{6,2},{1,5},{3,7},{5,1},{7,3},{8,12},{10,14},{12... | collective-permute-start | bytes 589832 | tf_op jit(solution)/shard_map/ppermute | solution.py:255
  43.0 1.6 %collective-permute-start.22 = (bf16[2,64,768]{2,1,0:T(8,128)(2,1)S(1)}, bf16[2,64,768]{2,1,0:T(8,128)(2,1)S(1)}, u32[]{:S(2)}, u32[]{:S(2)}) collective-permute-start(bf16[2,64,768]{2,1,0:T(8,128)(2,1)S(1)} %pad_maximum_fusion.7.refs_6_), channel_id=1, source_target_pairs={{0,2},{2,0},{4,6},{6,4},{1,3},{3,1},{5,7},{7,5},{8,10},{10,8},{12,... | collective-permute-start | bytes 589832 | tf_op jit(solution)/shard_map/ppermute | solution.py:255
  44.5 5.0 %terms.7 = (bf16[3,4096,512]{2,1,0:T(8,128)(2,1)S(1)}, bf16[4,64,1024]{2,1,0:T(8,128)(2,1)S(1)}, bf16[2,64,1024]{2,1,0:T(8,128)(2,1)S(1)}, bf16[1,64,1024]{2,1,0:T(8,128)(2,1)S(1)}, bf16[1,64,1024]{2,1,0:T(8,128)(2,1)S(1)}) custom-call(s32[1,4]{1,0:T(1,128)S(1)} %copy-done, ...), custom_call_target="tpu_custom_call", output_to_operand_aliasing={{0}: (2, {})} | custom-call | flops 4294967296 | bytes 8388608 | tf_op jit(solution)/shard_map/terms/pallas_call | solution.py:227
  49.6 0.1 collective-permute-start.26
  49.7 0.5 collective-permute-start.21
  50.2 0.1 collective-permute-start.25
  50.3 0.1 convert_element_type.554
  50.4 0.2 fusion.13
  50.7 0.3 collective-permute-done.26
  51.0 8.0 %collective-permute-start.17 = (bf16[64,2048]{1,0:T(8,128)(2,1)S(1)}, bf16[64,2048]{1,0:T(8,128)(2,1)S(1)}, u32[]{:S(2)}, u32[]{:S(2)}) collective-permute-start(bf16[64,2048]{1,0:T(8,128)(2,1)S(1)} %pad_maximum_fusion.2), channel_id=1, source_target_pairs={{0,24},{8,0},{16,8},{24,16},{1,25},{9,1},{17,9},{25,17},{2,26},{10... | collective-permute-start | bytes 786440 | tf_op jit(solution)/shard_map/ppermute | solution.py:260
  59.0 0.1 fusion.68
  59.1 0.1 collective-permute-start.27
  59.2 1.2 %collective-permute-start.29 = (bf16[2,64,512]{2,1,0:T(8,128)(2,1)S(1)}, bf16[2,64,512]{2,1,0:T(8,128)(2,1)S(1)}, u32[]{:S(2)}, u32[]{:S(2)}) collective-permute-start(bf16[2,64,512]{2,1,0:T(8,128)(2,1)S(1)} %pad_maximum_fusion.10), channel_id=1, source_target_pairs={{0,2},{2,0},{4,6},{6,4},{1,3},{3,1},{5,7},{7,5},{8,10},{10,8},{12,... | collective-permute-start | bytes 393224 | tf_op jit(solution)/shard_map/ppermute | solution.py:255
  60.4 0.1 fusion.26
  60.5 1.0 %collective-permute-start.20 = (bf16[64,768]{1,0:T(8,128)(2,1)S(1)}, bf16[64,768]{1,0:T(8,128)(2,1)S(1)}, u32[]{:S(2)}, u32[]{:S(2)}) collective-permute-start(bf16[64,768]{1,0:T(8,128)(2,1)S(1)} %get-tuple-element.51), channel_id=1, source_target_pairs={{0,2},{2,0},{4,6},{6,4},{1,3},{3,1},{5,7},{7,5},{8,10},{10,8},{12,... | collective-permute-start | bytes 294920 | tf_op jit(solution)/shard_map/ppermute | solution.py:255
  61.5 2.0 %collective-permute-start.23 = (bf16[64,768]{1,0:T(8,128)(2,1)S(1)}, bf16[64,768]{1,0:T(8,128)(2,1)S(1)}, u32[]{:S(2)}, u32[]{:S(2)}) collective-permute-start(bf16[64,768]{1,0:T(8,128)(2,1)S(1)} %get-tuple-element.52), channel_id=1, source_target_pairs={{0,4},{2,6},{4,0},{6,2},{1,5},{3,7},{5,1},{7,3},{8,12},{10,14},{12... | collective-permute-start | bytes 294920 | tf_op jit(solution)/shard_map/ppermute | solution.py:255
  63.5 2.0 %collective-permute-done.27 = bf16[2,64,512]{2,1,0:T(8,128)(2,1)S(1)} collective-permute-done((bf16[2,64,512]{2,1,0:T(8,128)(2,1)S(1)}, bf16[2,64,512]{2,1,0:T(8,128)(2,1)S(1)}, u32[]{:S(2)}, u32[]{:S(2)}) %collective-permute-start.27) | collective-permute-done | bytes 131104 | tf_op jit(solution)/shard_map/ppermute | solution.py:255
  65.5 0.1 collective-permute-done.29
  65.7 0.9 %collective-permute-start.28 = (bf16[64,512]{1,0:T(8,128)(2,1)S(1)}, bf16[64,512]{1,0:T(8,128)(2,1)S(1)}, u32[]{:S(2)}, u32[]{:S(2)}) collective-permute-start(bf16[64,512]{1,0:T(8,128)(2,1)S(1)} %get-tuple-element.77), channel_id=1, source_target_pairs={{0,2},{2,0},{4,6},{6,4},{1,3},{3,1},{5,7},{7,5},{8,10},{10,8},{12,... | collective-permute-start | bytes 196616 | tf_op jit(solution)/shard_map/ppermute | solution.py:255
  66.6 1.4 %collective-permute-start.30 = (bf16[64,512]{1,0:T(8,128)(2,1)S(1)}, bf16[64,512]{1,0:T(8,128)(2,1)S(1)}, u32[]{:S(2)}, u32[]{:S(2)}) collective-permute-start(bf16[64,512]{1,0:T(8,128)(2,1)S(1)} %get-tuple-element.78), channel_id=1, source_target_pairs={{0,4},{2,6},{4,0},{6,2},{1,5},{3,7},{5,1},{7,3},{8,12},{10,14},{12... | collective-permute-start | bytes 196616 | tf_op jit(solution)/shard_map/ppermute | solution.py:255
  68.0 0.1 fusion.29
  68.1 1.7 %collective-permute-start.24 = (bf16[64,1536]{1,0:T(8,128)(2,1)S(1)}, bf16[64,1536]{1,0:T(8,128)(2,1)S(1)}, u32[]{:S(2)}, u32[]{:S(2)}) collective-permute-start(bf16[64,1536]{1,0:T(8,128)(2,1)S(1)} %pad_maximum_fusion.8), channel_id=1, source_target_pairs={{0,24},{8,0},{16,8},{24,16},{1,25},{9,1},{17,9},{25,17},{2,26},{10... | collective-permute-start | bytes 589832 | tf_op jit(solution)/shard_map/ppermute | solution.py:260
  69.9 0.1 collective-permute-done.28
  70.0 0.9 %collective-permute-done.30 = bf16[64,512]{1,0:T(8,128)(2,1)S(1)} collective-permute-done((bf16[64,512]{1,0:T(8,128)(2,1)S(1)}, bf16[64,512]{1,0:T(8,128)(2,1)S(1)}, u32[]{:S(2)}, u32[]{:S(2)}) %collective-permute-start.30) | collective-permute-done | bytes 65568 | tf_op jit(solution)/shard_map/ppermute | solution.py:255
  70.9 0.1 fusion.66
  71.0 1.4 %collective-permute-start.31 = (bf16[64,1024]{1,0:T(8,128)(2,1)S(1)}, bf16[64,1024]{1,0:T(8,128)(2,1)S(1)}, u32[]{:S(2)}, u32[]{:S(2)}) collective-permute-start(bf16[64,1024]{1,0:T(8,128)(2,1)S(1)} %pad_maximum_fusion.11), channel_id=1, source_target_pairs={{0,24},{8,0},{16,8},{24,16},{1,25},{9,1},{17,9},{25,17},{2,26},{10... | collective-permute-start | bytes 393224 | tf_op jit(solution)/shard_map/ppermute | solution.py:260
  72.4 3.6 %collective-permute-done.31 = bf16[64,1024]{1,0:T(8,128)(2,1)S(1)} collective-permute-done((bf16[64,1024]{1,0:T(8,128)(2,1)S(1)}, bf16[64,1024]{1,0:T(8,128)(2,1)S(1)}, u32[]{:S(2)}, u32[]{:S(2)}) %collective-permute-start.31) | collective-permute-done | bytes 131104 | tf_op jit(solution)/shard_map/ppermute | solution.py:260
  76.0 0.9 %maximum_bitcast_fusion = bf16[1,64,6144]{2,1,0:T(8,128)(2,1)} fusion(bf16[64,1024]{1,0:T(8,128)(2,1)S(1)} %collective-permute-done.31, bf16[64,1536]{1,0:T(8,128)(2,1)S(1)} %collective-permute-done.24, bf16[64,2048]{1,0:T(8,128)(2,1)S(1)} %collective-permute-done.17, bf16[64,1536]{1,0:T(8,128)(2,1)S(1)} %collective-permute-done.9), kind=kLoop, calls=%fused_computation | loop fusion | flops 3145728 | bytes 1572864 | tf_op jit(solution)/shard_map/broadcast_in_dim | solution.py:355
  (44 shorter events, 0.5 us)
Async XLA Ops:
  0.0 0.7 copy-start
  11.4 1.6 %collective-permute-start.1 = (bf16[1,64,1536]{2,1,0:T(8,128)(2,1)S(1)}, bf16[1,64,1536]{2,1,0:T(8,128)(2,1)S(1)}, u32[]{:S(2)}, u32[]{:S(2)}) collective-permute-start(bf16[1,64,1536]{2,1,0:T(8,128)(2,1)S(1)} %get-tuple-element.27), channel_id=1, source_target_pairs={{0,1},{1,0},{2,3},{3,2},{4,5},{5,4},{6,7},{7,6},{8,9},{9,8},{10,11... | collective-permute-start | bytes 589832 | tf_op jit(solution)/shard_map/ppermute | solution.py:255
  11.9 1.4 %collective-permute-start.2 = (bf16[1,64,1536]{2,1,0:T(8,128)(2,1)S(1)}, bf16[1,64,1536]{2,1,0:T(8,128)(2,1)S(1)}, u32[]{:S(2)}, u32[]{:S(2)}) collective-permute-start(bf16[1,64,1536]{2,1,0:T(8,128)(2,1)S(1)} %get-tuple-element.28), channel_id=1, source_target_pairs={{0,1},{1,0},{2,3},{3,2},{4,5},{5,4},{6,7},{7,6},{8,9},{9,8},{10,11... | collective-permute-start | bytes 589832 | tf_op jit(solution)/shard_map/ppermute | solution.py:255
  12.0 14.6 %collective-permute-start = (bf16[2,64,1536]{2,1,0:T(8,128)(2,1)S(1)}, bf16[2,64,1536]{2,1,0:T(8,128)(2,1)S(1)}, u32[]{:S(2)}, u32[]{:S(2)}) collective-permute-start(bf16[2,64,1536]{2,1,0:T(8,128)(2,1)S(1)} %get-tuple-element.26), channel_id=1, source_target_pairs={{0,1},{1,0},{2,3},{3,2},{4,5},{5,4},{6,7},{7,6},{8,9},{9,8},{10,11... | collective-permute-start | bytes 1179656 | tf_op jit(solution)/shard_map/ppermute | solution.py:255
  13.5 12.8 %collective-permute-start.3 = (bf16[2,64,768]{2,1,0:T(8,128)(2,1)S(1)}, bf16[2,64,768]{2,1,0:T(8,128)(2,1)S(1)}, u32[]{:S(2)}, u32[]{:S(2)}) collective-permute-start(bf16[2,64,768]{2,1,0:T(8,128)(2,1)S(1)} %pad_maximum_fusion.3.refs_5_), channel_id=1, source_target_pairs={{0,4},{2,6},{4,0},{6,2},{1,5},{3,7},{5,1},{7,3},{8,12},{10,14},{12... | collective-permute-start | bytes 589832 | tf_op jit(solution)/shard_map/ppermute | solution.py:255
  13.6 12.7 %collective-permute-start.5 = (bf16[2,64,768]{2,1,0:T(8,128)(2,1)S(1)}, bf16[2,64,768]{2,1,0:T(8,128)(2,1)S(1)}, u32[]{:S(2)}, u32[]{:S(2)}) collective-permute-start(bf16[2,64,768]{2,1,0:T(8,128)(2,1)S(1)} %pad_maximum_fusion.4.refs_6_), channel_id=1, source_target_pairs={{0,2},{2,0},{4,6},{6,4},{1,3},{3,1},{5,7},{7,5},{8,10},{10,8},{12,... | collective-permute-start | bytes 589832 | tf_op jit(solution)/shard_map/ppermute | solution.py:255
  25.8 1.6 %collective-permute-start.7 = (bf16[1,64,2048]{2,1,0:T(8,128)(2,1)S(1)}, bf16[1,64,2048]{2,1,0:T(8,128)(2,1)S(1)}, u32[]{:S(2)}, u32[]{:S(2)}) collective-permute-start(bf16[1,64,2048]{2,1,0:T(8,128)(2,1)S(1)} %get-tuple-element.34), channel_id=1, source_target_pairs={{0,1},{1,0},{2,3},{3,2},{4,5},{5,4},{6,7},{7,6},{8,9},{9,8},{10,11... | collective-permute-start | bytes 786440 | tf_op jit(solution)/shard_map/ppermute | solution.py:255
  25.8 13.5 %collective-permute-start.10 = (bf16[2,64,2048]{2,1,0:T(8,128)(2,1)S(1)}, bf16[2,64,2048]{2,1,0:T(8,128)(2,1)S(1)}, u32[]{:S(2)}, u32[]{:S(2)}) collective-permute-start(bf16[2,64,2048]{2,1,0:T(8,128)(2,1)S(1)} %get-tuple-element.36), channel_id=1, source_target_pairs={{0,1},{1,0},{2,3},{3,2},{4,5},{5,4},{6,7},{7,6},{8,9},{9,8},{10,11... | collective-permute-start | bytes 1572872 | tf_op jit(solution)/shard_map/ppermute | solution.py:255
  26.4 2.0 %collective-permute-start.6 = (bf16[1,64,2048]{2,1,0:T(8,128)(2,1)S(1)}, bf16[1,64,2048]{2,1,0:T(8,128)(2,1)S(1)}, u32[]{:S(2)}, u32[]{:S(2)}) collective-permute-start(bf16[1,64,2048]{2,1,0:T(8,128)(2,1)S(1)} %bitcast_add_fusion), channel_id=1, source_target_pairs={{0,1},{1,0},{2,3},{3,2},{4,5},{5,4},{6,7},{7,6},{8,9},{9,8},{10,11... | collective-permute-start | bytes 786440 | tf_op jit(solution)/shard_map/ppermute | solution.py:255
  26.7 11.9 %collective-permute-start.4 = (bf16[64,768]{1,0:T(8,128)(2,1)S(1)}, bf16[64,768]{1,0:T(8,128)(2,1)S(1)}, u32[]{:S(2)}, u32[]{:S(2)}) collective-permute-start(bf16[64,768]{1,0:T(8,128)(2,1)S(1)} %get-tuple-element.53), channel_id=1, source_target_pairs={{0,2},{2,0},{4,6},{6,4},{1,3},{3,1},{5,7},{7,5},{8,10},{10,8},{12,... | collective-permute-start | bytes 294920 | tf_op jit(solution)/shard_map/ppermute | solution.py:255
  27.0 11.7 %collective-permute-start.8 = (bf16[64,768]{1,0:T(8,128)(2,1)S(1)}, bf16[64,768]{1,0:T(8,128)(2,1)S(1)}, u32[]{:S(2)}, u32[]{:S(2)}) collective-permute-start(bf16[64,768]{1,0:T(8,128)(2,1)S(1)} %get-tuple-element.54), channel_id=1, source_target_pairs={{0,4},{2,6},{4,0},{6,2},{1,5},{3,7},{5,1},{7,3},{8,12},{10,14},{12... | collective-permute-start | bytes 294920 | tf_op jit(solution)/shard_map/ppermute | solution.py:255
  28.7 10.9 %collective-permute-start.11 = (bf16[2,64,1024]{2,1,0:T(8,128)(2,1)S(1)}, bf16[2,64,1024]{2,1,0:T(8,128)(2,1)S(1)}, u32[]{:S(2)}, u32[]{:S(2)}) collective-permute-start(bf16[2,64,1024]{2,1,0:T(8,128)(2,1)S(1)} %pad_maximum_fusion.refs_5_), channel_id=1, source_target_pairs={{0,4},{2,6},{4,0},{6,2},{1,5},{3,7},{5,1},{7,3},{8,12},{10,14},{12... | collective-permute-start | bytes 786440 | tf_op jit(solution)/shard_map/ppermute | solution.py:255
  29.3 10.3 %collective-permute-start.13 = (bf16[2,64,1024]{2,1,0:T(8,128)(2,1)S(1)}, bf16[2,64,1024]{2,1,0:T(8,128)(2,1)S(1)}, u32[]{:S(2)}, u32[]{:S(2)}) collective-permute-start(bf16[2,64,1024]{2,1,0:T(8,128)(2,1)S(1)} %pad_maximum_fusion.1.refs_6_), channel_id=1, source_target_pairs={{0,2},{2,0},{4,6},{6,4},{1,3},{3,1},{5,7},{7,5},{8,10},{10,8},{12,... | collective-permute-start | bytes 786440 | tf_op jit(solution)/shard_map/ppermute | solution.py:255
  38.6 2.2 %collective-permute-start.15 = (bf16[1,64,1536]{2,1,0:T(8,128)(2,1)S(1)}, bf16[1,64,1536]{2,1,0:T(8,128)(2,1)S(1)}, u32[]{:S(2)}, u32[]{:S(2)}) collective-permute-start(bf16[1,64,1536]{2,1,0:T(8,128)(2,1)S(1)} %get-tuple-element.39), channel_id=1, source_target_pairs={{0,1},{1,0},{2,3},{3,2},{4,5},{5,4},{6,7},{7,6},{8,9},{9,8},{10,11... | collective-permute-start | bytes 589832 | tf_op jit(solution)/shard_map/ppermute | solution.py:255
  38.7 2.0 %collective-permute-start.18 = (bf16[2,64,1536]{2,1,0:T(8,128)(2,1)S(1)}, bf16[2,64,1536]{2,1,0:T(8,128)(2,1)S(1)}, u32[]{:S(2)}, u32[]{:S(2)}) collective-permute-start(bf16[2,64,1536]{2,1,0:T(8,128)(2,1)S(1)} %get-tuple-element.41), channel_id=1, source_target_pairs={{0,1},{1,0},{2,3},{3,2},{4,5},{5,4},{6,7},{7,6},{8,9},{9,8},{10,11... | collective-permute-start | bytes 1179656 | tf_op jit(solution)/shard_map/ppermute | solution.py:255
  39.3 10.2 %collective-permute-start.9 = (bf16[64,1536]{1,0:T(8,128)(2,1)S(1)}, bf16[64,1536]{1,0:T(8,128)(2,1)S(1)}, u32[]{:S(2)}, u32[]{:S(2)}) collective-permute-start(bf16[64,1536]{1,0:T(8,128)(2,1)S(1)} %pad_maximum_fusion.5.refs_7_), channel_id=1, source_target_pairs={{0,24},{8,0},{16,8},{24,16},{1,25},{9,1},{17,9},{25,17},{2,26},{10... | collective-permute-start | bytes 589832 | tf_op jit(solution)/shard_map/ppermute | solution.py:260
  39.8 1.5 %collective-permute-start.14 = (bf16[1,64,1536]{2,1,0:T(8,128)(2,1)S(1)}, bf16[1,64,1536]{2,1,0:T(8,128)(2,1)S(1)}, u32[]{:S(2)}, u32[]{:S(2)}) collective-permute-start(bf16[1,64,1536]{2,1,0:T(8,128)(2,1)S(1)} %bitcast_add_fusion.2), channel_id=1, source_target_pairs={{0,1},{1,0},{2,3},{3,2},{4,5},{5,4},{6,7},{7,6},{8,9},{9,8},{10,11... | collective-permute-start | bytes 589832 | tf_op jit(solution)/shard_map/ppermute | solution.py:255
  40.1 9.5 %collective-permute-start.12 = (bf16[64,1024]{1,0:T(8,128)(2,1)S(1)}, bf16[64,1024]{1,0:T(8,128)(2,1)S(1)}, u32[]{:S(2)}, u32[]{:S(2)}) collective-permute-start(bf16[64,1024]{1,0:T(8,128)(2,1)S(1)} %get-tuple-element.45), channel_id=1, source_target_pairs={{0,2},{2,0},{4,6},{6,4},{1,3},{3,1},{5,7},{7,5},{8,10},{10,8},{12,... | collective-permute-start | bytes 393224 | tf_op jit(solution)/shard_map/ppermute | solution.py:255
  40.7 9.0 %collective-permute-start.16 = (bf16[64,1024]{1,0:T(8,128)(2,1)S(1)}, bf16[64,1024]{1,0:T(8,128)(2,1)S(1)}, u32[]{:S(2)}, u32[]{:S(2)}) collective-permute-start(bf16[64,1024]{1,0:T(8,128)(2,1)S(1)} %get-tuple-element.46), channel_id=1, source_target_pairs={{0,4},{2,6},{4,0},{6,2},{1,5},{3,7},{5,1},{7,3},{8,12},{10,14},{12... | collective-permute-start | bytes 393224 | tf_op jit(solution)/shard_map/ppermute | solution.py:255
  41.4 17.8 %collective-permute-start.19 = (bf16[2,64,768]{2,1,0:T(8,128)(2,1)S(1)}, bf16[2,64,768]{2,1,0:T(8,128)(2,1)S(1)}, u32[]{:S(2)}, u32[]{:S(2)}) collective-permute-start(bf16[2,64,768]{2,1,0:T(8,128)(2,1)S(1)} %pad_maximum_fusion.6.refs_5_), channel_id=1, source_target_pairs={{0,4},{2,6},{4,0},{6,2},{1,5},{3,7},{5,1},{7,3},{8,12},{10,14},{12... | collective-permute-start | bytes 589832 | tf_op jit(solution)/shard_map/ppermute | solution.py:255
  43.0 17.4 %collective-permute-start.22 = (bf16[2,64,768]{2,1,0:T(8,128)(2,1)S(1)}, bf16[2,64,768]{2,1,0:T(8,128)(2,1)S(1)}, u32[]{:S(2)}, u32[]{:S(2)}) collective-permute-start(bf16[2,64,768]{2,1,0:T(8,128)(2,1)S(1)} %pad_maximum_fusion.7.refs_6_), channel_id=1, source_target_pairs={{0,2},{2,0},{4,6},{6,4},{1,3},{3,1},{5,7},{7,5},{8,10},{10,8},{12,... | collective-permute-start | bytes 589832 | tf_op jit(solution)/shard_map/ppermute | solution.py:255
  49.6 1.4 %collective-permute-start.26 = (bf16[1,64,1024]{2,1,0:T(8,128)(2,1)S(1)}, bf16[1,64,1024]{2,1,0:T(8,128)(2,1)S(1)}, u32[]{:S(2)}, u32[]{:S(2)}) collective-permute-start(bf16[1,64,1024]{2,1,0:T(8,128)(2,1)S(1)} %get-tuple-element.44), channel_id=1, source_target_pairs={{0,1},{1,0},{2,3},{3,2},{4,5},{5,4},{6,7},{7,6},{8,9},{9,8},{10,11... | collective-permute-start | bytes 393224 | tf_op jit(solution)/shard_map/ppermute | solution.py:255
  49.7 9.3 %collective-permute-start.21 = (bf16[1,64,1024]{2,1,0:T(8,128)(2,1)S(1)}, bf16[1,64,1024]{2,1,0:T(8,128)(2,1)S(1)}, u32[]{:S(2)}, u32[]{:S(2)}) collective-permute-start(bf16[1,64,1024]{2,1,0:T(8,128)(2,1)S(1)} %fusion.56), channel_id=1, source_target_pairs={{0,1},{1,0},{2,3},{3,2},{4,5},{5,4},{6,7},{7,6},{8,9},{9,8},{10,11... | collective-permute-start | bytes 393224 | tf_op jit(solution)/shard_map/ppermute | solution.py:255
  50.2 11.2 %collective-permute-start.25 = (bf16[2,64,1024]{2,1,0:T(8,128)(2,1)S(1)}, bf16[2,64,1024]{2,1,0:T(8,128)(2,1)S(1)}, u32[]{:S(2)}, u32[]{:S(2)}) collective-permute-start(bf16[2,64,1024]{2,1,0:T(8,128)(2,1)S(1)} %get-tuple-element.43), channel_id=1, source_target_pairs={{0,1},{1,0},{2,3},{3,2},{4,5},{5,4},{6,7},{7,6},{8,9},{9,8},{10,11... | collective-permute-start | bytes 786440 | tf_op jit(solution)/shard_map/ppermute | solution.py:255
  51.0 18.9 %collective-permute-start.17 = (bf16[64,2048]{1,0:T(8,128)(2,1)S(1)}, bf16[64,2048]{1,0:T(8,128)(2,1)S(1)}, u32[]{:S(2)}, u32[]{:S(2)}) collective-permute-start(bf16[64,2048]{1,0:T(8,128)(2,1)S(1)} %pad_maximum_fusion.2), channel_id=1, source_target_pairs={{0,24},{8,0},{16,8},{24,16},{1,25},{9,1},{17,9},{25,17},{2,26},{10... | collective-permute-start | bytes 786440 | tf_op jit(solution)/shard_map/ppermute | solution.py:260
  59.1 6.4 %collective-permute-start.27 = (bf16[2,64,512]{2,1,0:T(8,128)(2,1)S(1)}, bf16[2,64,512]{2,1,0:T(8,128)(2,1)S(1)}, u32[]{:S(2)}, u32[]{:S(2)}) collective-permute-start(bf16[2,64,512]{2,1,0:T(8,128)(2,1)S(1)} %pad_maximum_fusion.9), channel_id=1, source_target_pairs={{0,4},{2,6},{4,0},{6,2},{1,5},{3,7},{5,1},{7,3},{8,12},{10,14},{12... | collective-permute-start | bytes 393224 | tf_op jit(solution)/shard_map/ppermute | solution.py:255
  59.2 6.4 %collective-permute-start.29 = (bf16[2,64,512]{2,1,0:T(8,128)(2,1)S(1)}, bf16[2,64,512]{2,1,0:T(8,128)(2,1)S(1)}, u32[]{:S(2)}, u32[]{:S(2)}) collective-permute-start(bf16[2,64,512]{2,1,0:T(8,128)(2,1)S(1)} %pad_maximum_fusion.10), channel_id=1, source_target_pairs={{0,2},{2,0},{4,6},{6,4},{1,3},{3,1},{5,7},{7,5},{8,10},{10,8},{12,... | collective-permute-start | bytes 393224 | tf_op jit(solution)/shard_map/ppermute | solution.py:255
  60.5 7.5 %collective-permute-start.20 = (bf16[64,768]{1,0:T(8,128)(2,1)S(1)}, bf16[64,768]{1,0:T(8,128)(2,1)S(1)}, u32[]{:S(2)}, u32[]{:S(2)}) collective-permute-start(bf16[64,768]{1,0:T(8,128)(2,1)S(1)} %get-tuple-element.51), channel_id=1, source_target_pairs={{0,2},{2,0},{4,6},{6,4},{1,3},{3,1},{5,7},{7,5},{8,10},{10,8},{12,... | collective-permute-start | bytes 294920 | tf_op jit(solution)/shard_map/ppermute | solution.py:255
  61.5 6.5 %collective-permute-start.23 = (bf16[64,768]{1,0:T(8,128)(2,1)S(1)}, bf16[64,768]{1,0:T(8,128)(2,1)S(1)}, u32[]{:S(2)}, u32[]{:S(2)}) collective-permute-start(bf16[64,768]{1,0:T(8,128)(2,1)S(1)} %get-tuple-element.52), channel_id=1, source_target_pairs={{0,4},{2,6},{4,0},{6,2},{1,5},{3,7},{5,1},{7,3},{8,12},{10,14},{12... | collective-permute-start | bytes 294920 | tf_op jit(solution)/shard_map/ppermute | solution.py:255
  65.7 4.3 %collective-permute-start.28 = (bf16[64,512]{1,0:T(8,128)(2,1)S(1)}, bf16[64,512]{1,0:T(8,128)(2,1)S(1)}, u32[]{:S(2)}, u32[]{:S(2)}) collective-permute-start(bf16[64,512]{1,0:T(8,128)(2,1)S(1)} %get-tuple-element.77), channel_id=1, source_target_pairs={{0,2},{2,0},{4,6},{6,4},{1,3},{3,1},{5,7},{7,5},{8,10},{10,8},{12,... | collective-permute-start | bytes 196616 | tf_op jit(solution)/shard_map/ppermute | solution.py:255
  66.6 4.3 %collective-permute-start.30 = (bf16[64,512]{1,0:T(8,128)(2,1)S(1)}, bf16[64,512]{1,0:T(8,128)(2,1)S(1)}, u32[]{:S(2)}, u32[]{:S(2)}) collective-permute-start(bf16[64,512]{1,0:T(8,128)(2,1)S(1)} %get-tuple-element.78), channel_id=1, source_target_pairs={{0,4},{2,6},{4,0},{6,2},{1,5},{3,7},{5,1},{7,3},{8,12},{10,14},{12... | collective-permute-start | bytes 196616 | tf_op jit(solution)/shard_map/ppermute | solution.py:255
  68.1 7.8 %collective-permute-start.24 = (bf16[64,1536]{1,0:T(8,128)(2,1)S(1)}, bf16[64,1536]{1,0:T(8,128)(2,1)S(1)}, u32[]{:S(2)}, u32[]{:S(2)}) collective-permute-start(bf16[64,1536]{1,0:T(8,128)(2,1)S(1)} %pad_maximum_fusion.8), channel_id=1, source_target_pairs={{0,24},{8,0},{16,8},{24,16},{1,25},{9,1},{17,9},{25,17},{2,26},{10... | collective-permute-start | bytes 589832 | tf_op jit(solution)/shard_map/ppermute | solution.py:260
  71.0 5.0 %collective-permute-start.31 = (bf16[64,1024]{1,0:T(8,128)(2,1)S(1)}, bf16[64,1024]{1,0:T(8,128)(2,1)S(1)}, u32[]{:S(2)}, u32[]{:S(2)}) collective-permute-start(bf16[64,1024]{1,0:T(8,128)(2,1)S(1)} %pad_maximum_fusion.11), channel_id=1, source_target_pairs={{0,24},{8,0},{16,8},{24,16},{1,25},{9,1},{17,9},{25,17},{2,26},{10... | collective-permute-start | bytes 393224 | tf_op jit(solution)/shard_map/ppermute | solution.py:260
